TPU v7x, 32 devices: a whole 2x2x4 slice. The times are simulated.
32 devices in a mesh: blk: 8 (over y, x, core), off: 4 (over z).
Axes of the slice: x: 2, y: 2, z: 4, core: 2. Of those that a mesh axis runs over, the one named last changes fastest.
Arguments:
- coefficients: bfloat16 [128, 32, 128], P('blk', 'off'), may hold values from -12 to 12
Outputs:
- smoothed: float32 [128, 32, 128], P(('blk', 'off'))
- log_degree: float32 [128], P(('blk', 'off'))
All inputs are finite; a program needn't handle non-finite values.
Results may differ from a plain program's by a relative error of at most 0.005.
Values may be sent and summed in bfloat16 or wider, within the bound.
No kernel may reach another device: no remote copies, remote signals or barrier semaphores. Data moves between devices by JAX's collectives and lax.ppermute only.
A program may use at most 64 MiB of HBM per device.

v0:
```python
import math
import jax
import jax.numpy as jnp
from jax import lax
from jax.sharding import PartitionSpec as P

epsilon = 1e-06
concentration = 40.0


def shifted(array, axis, by):
    count = lax.axis_size(axis)
    return lax.ppermute(array, axis, [(i, (i + by) % count) for i in range(count)])


def angle_tables(angular):
    half_width = angular // 2
    frequency = jnp.arange(half_width, dtype=jnp.int32)
    shifts = jnp.arange(angular, dtype=jnp.int32)
    product = frequency[:, None] * shifts[None, :] % angular
    phase = product.astype(jnp.float32) * (2.0 * math.pi / angular)
    forward = jnp.concatenate([jnp.cos(phase), -jnp.sin(phase)], axis=0)
    return (forward, forward.T)


def inverse_norms(block_values):
    values = block_values.astype(jnp.float32)
    return lax.rsqrt(jnp.sum(values * values, axis=(1, 2)) + epsilon)


def tile_terms(own_block, own_inverse, other_block, offset, forward, backward):
    row_count = own_block.shape[0]
    half_width = own_block.shape[2] // 2
    highest = lax.Precision.HIGHEST
    other_inverse = inverse_norms(other_block)
    swapped = jnp.concatenate(
        [other_block[:, :, half_width:], other_block[:, :, :half_width]], axis=2
    )
    direct = jnp.einsum("irc,jrc->ijc", own_block, other_block, preferred_element_type=jnp.float32)
    mixed_terms = jnp.einsum("irc,jrc->ijc", own_block, swapped, preferred_element_type=jnp.float32)
    real_part = direct[:, :, :half_width] + direct[:, :, half_width:]
    imag_part = mixed_terms[:, :, half_width:] - mixed_terms[:, :, :half_width]
    cross_spectrum = jnp.concatenate([real_part, imag_part], axis=2).reshape(
        row_count * row_count, -1
    )
    correlation = jnp.dot(
        cross_spectrum, forward, precision=highest, preferred_element_type=jnp.float32
    )
    correlation = correlation.reshape(row_count, row_count, -1)
    cosine = correlation * own_inverse[:, None, None] * other_inverse[None, :, None]
    same_image = jnp.arange(row_count)[:, None] == jnp.arange(row_count)[None, :]
    keep_mask = jnp.where(jnp.logical_and(offset == 0, same_image), 0.0, 1.0).astype(jnp.float32)
    weights = jnp.exp(concentration * cosine) * keep_mask[:, :, None]
    spectral = jnp.dot(
        weights.reshape(row_count * row_count, -1),
        backward,
        precision=highest,
        preferred_element_type=jnp.float32,
    ).reshape(row_count, row_count, -1)
    degree = jnp.sum(spectral[:, :, 0], axis=1)
    rounded = spectral.astype(jnp.bfloat16)
    weight_real = jnp.concatenate([rounded[:, :, :half_width], rounded[:, :, :half_width]], axis=2)
    weight_imag = jnp.concatenate([-rounded[:, :, half_width:], rounded[:, :, half_width:]], axis=2)
    filtered = jnp.einsum(
        "ijc,jrc->irc", weight_real, other_block, preferred_element_type=jnp.float32
    )
    filtered = filtered + jnp.einsum(
        "ijc,jrc->irc", weight_imag, swapped, preferred_element_type=jnp.float32
    )
    return (filtered, degree)


def body(coefficients):
    own_block = lax.all_gather(coefficients, "off", axis=1, tiled=True)
    own_inverse = inverse_norms(own_block)
    row_count, radial, angular = own_block.shape
    forward, backward = angle_tables(angular)
    ranges = lax.axis_size("off")
    per_range = min(8, lax.axis_size("blk") // ranges)
    range_index = lax.axis_index("off")
    range_base = range_index * per_range
    packet = own_block
    packet = shifted(packet, "blk", -(per_range // 2))
    for bit_number in range(ranges.bit_length() - 1):
        moved_packet = shifted(packet, "blk", -(per_range << bit_number))
        chosen = range_index // (1 << bit_number) % 2 == 1
        packet = jnp.where(chosen, moved_packet, packet)
    empty_sum = jnp.zeros((row_count, radial, angular), jnp.float32)
    empty_degree = jnp.zeros((row_count,), jnp.float32)
    centre = range_base + per_range // 2
    lower_block = shifted(packet, "blk", 1)

    def advance_both(step, loop_state):
        filtered, degree, upper_block, lower_part = loop_state
        upper_terms = tile_terms(
            own_block, own_inverse, upper_block, centre + step, forward, backward
        )
        lower_terms = tile_terms(
            own_block, own_inverse, lower_part, centre - 1 - step, forward, backward
        )
        upper_block = shifted(upper_block, "blk", -1)
        lower_part = shifted(lower_part, "blk", 1)
        return (
            filtered + upper_terms[0] + lower_terms[0],
            degree + upper_terms[1] + lower_terms[1],
            upper_block,
            lower_part,
        )

    last_step = per_range // 2 - 1
    filtered, degree, upper_block, lower_block = lax.fori_loop(
        0, last_step, advance_both, (empty_sum, empty_degree, packet, lower_block)
    )
    upper_terms = tile_terms(
        own_block, own_inverse, upper_block, centre + last_step, forward, backward
    )
    lower_terms = tile_terms(
        own_block, own_inverse, lower_block, centre - 1 - last_step, forward, backward
    )
    filtered = filtered + upper_terms[0] + lower_terms[0]
    degree = degree + upper_terms[1] + lower_terms[1]
    totals = (
        lax.psum_scatter(filtered, "off", scatter_dimension=0, tiled=True),
        lax.psum_scatter(degree, "off", scatter_dimension=0, tiled=True),
    )
    smoothed = totals[0] / totals[1][:, None, None]
    return (smoothed, jnp.log(totals[1]))


def solution(mesh):
    return jax.shard_map(
        body,
        mesh=mesh,
        in_specs=(P("blk", "off", None),),
        out_specs=(P(("blk", "off"), None, None), P(("blk", "off"))),
        check_vma=False,
    )
```

profile of v0, /device:TPU:0, one launch (start us, length us, event | category | flops | bytes accessed | tf_op | source)
XLA Modules:
  0.0 91.2 jit_solution(6162711789580707457)
XLA Ops:
  7.2 1.0 %copy.17 = bf16[16,8,128]{0,1,2:T(8,128)(2,1)S(1)} copy(bf16[16,8,128]{2,1,0:T(8,128)(2,1)} %param.1) | data formatting | bytes 65536 | tf_op args[0]
  8.2 23.4 %all_gather.3 = bf16[16,32,128]{0,1,2:T(8,128)(2,1)S(1)} all-gather(bf16[16,8,128]{0,1,2:T(8,128)(2,1)S(1)} %copy.17), channel_id=1, replica_groups=mesh['blk'=8,'off'=4] {'off'}, dimensions={1}, use_global_device_ids=true | all-gather | bytes 163840 | tf_op jit(solution)/shard_map/all_gather | solution.py:74
  31.6 1.2 %copy.18 = bf16[16,32,128]{2,1,0:T(8,128)(2,1)S(1)} copy(bf16[16,32,128]{0,1,2:T(8,128)(2,1)S(1)} %all_gather.3) | data formatting | bytes 262144 | tf_op jit(solution)/shard_map/all_gather | solution.py:74
  32.8 1.2 %collective-permute-start = (bf16[16,32,128]{2,1,0:T(8,128)(2,1)S(1)}, bf16[16,32,128]{2,1,0:T(8,128)(2,1)S(1)}, u32[]{:S(2)}, u32[]{:S(2)}) collective-permute-start(bf16[16,32,128]{2,1,0:T(8,128)(2,1)S(1)} %copy.18), channel_id=1, source_target_pairs={{0,28},{4,0},{8,4},{12,8},{16,12},{20,16},{24,20},{28,24},{1,29},{... | collective-permute-start | bytes 393224 | tf_op jit(solution)/shard_map/ppermute | solution.py:13
  34.0 0.6 multiply_reduce_fusion
  34.5 2.0 %collective-permute-done = bf16[16,32,128]{2,1,0:T(8,128)(2,1)S(1)} collective-permute-done((bf16[16,32,128]{2,1,0:T(8,128)(2,1)S(1)}, bf16[16,32,128]{2,1,0:T(8,128)(2,1)S(1)}, u32[]{:S(2)}, u32[]{:S(2)}) %collective-permute-start) | collective-permute-done | bytes 131104 | tf_op jit(solution)/shard_map/ppermute | solution.py:13
  36.5 1.3 %collective-permute-start.1 = (bf16[16,32,128]{2,1,0:T(8,128)(2,1)S(1)}, bf16[16,32,128]{2,1,0:T(8,128)(2,1)S(1)}, u32[]{:S(2)}, u32[]{:S(2)}) collective-permute-start(bf16[16,32,128]{2,1,0:T(8,128)(2,1)S(1)} %collective-permute-done), channel_id=1, source_target_pairs={{0,24},{4,28},{8,0},{12,4},{16,8},{20,12},{24,16},{28,20},{1,25},{... | collective-permute-start | bytes 393224 | tf_op jit(solution)/shard_map/ppermute | solution.py:13
  37.9 4.7 %collective-permute-done.1 = bf16[16,32,128]{2,1,0:T(8,128)(2,1)S(1)} collective-permute-done((bf16[16,32,128]{2,1,0:T(8,128)(2,1)S(1)}, bf16[16,32,128]{2,1,0:T(8,128)(2,1)S(1)}, u32[]{:S(2)}, u32[]{:S(2)}) %collective-permute-start.1) | collective-permute-done | bytes 131104 | tf_op jit(solution)/shard_map/ppermute | solution.py:13
  42.5 0.3 collective-permute-start.2
  42.9 0.1 sine_negate_fusion
  43.0 4.8 %collective-permute-done.2 = bf16[16,32,128]{2,1,0:T(8,128)(2,1)S(1)} collective-permute-done((bf16[16,32,128]{2,1,0:T(8,128)(2,1)S(1)}, bf16[16,32,128]{2,1,0:T(8,128)(2,1)S(1)}, u32[]{:S(2)}, u32[]{:S(2)}) %collective-permute-start.2) | collective-permute-done | bytes 131104 | tf_op jit(solution)/shard_map/ppermute | solution.py:13
  47.8 0.2 multiply_reduce_fusion.2
  48.0 0.2 collective-permute-start.3
  48.3 0.4 copy.23
  48.9 0.4 copy.20
  49.3 0.4 convolution_bitcast_fusion.2
  49.8 0.3 copy.22
  50.1 0.4 convolution_bitcast_fusion.3
  50.6 0.3 copy.21
  50.9 0.3 fusion.5
  51.2 0.3 fusion.39
  51.7 0.4 copy.26
  52.1 1.4 %fusion.40 = f32[128,32,16]{1,2,0:T(8,128)} fusion(bf16[16,16,128]{1,0,2:T(8,128)(2,1)S(1)} %copy.26, bf16[16,32,128]{1,0,2:T(8,128)(2,1)S(1)} %copy.20), kind=kOutput, calls=%fused_computation.77 | convolution fusion | flops 2097152 | bytes 458752 | tf_op jit(solution)/shard_map/ijc,jrc->irc/dot_general | solution.py:67
  53.6 1.2 %copy.24 = bf16[16,16,128]{1,0,2:T(8,128)(2,1)} copy(bf16[16,16,128]{2,1,0:T(8,128)(2,1)S(1)} %pad_maximum_fusion.2) | data formatting | bytes 131072 | tf_op jit(solution)/shard_map/concatenate | solution.py:62
  55.1 0.4 copy.28
  55.5 0.4 convolution_bitcast_fusion
  56.0 0.3 copy.30
  56.3 0.4 copy.31
  56.7 0.4 convolution_bitcast_fusion.1
  57.2 0.3 copy.29
  57.5 0.2 multiply_reduce_fusion.1
  57.7 0.3 fusion.9
  58.0 0.3 fusion.38
  58.5 0.4 copy.34
  58.9 0.4 fusion.41
  59.4 0.4 copy.32
  59.9 0.4 convolution_add_fusion
  60.3 0.8 copy-done
  61.1 0.1 copy-done.1
  61.2 0.4 fusion.1
  61.6 1.1 %copy.35 = f32[16,32,128]{2,1,0:T(8,128)} copy(f32[16,32,128]{1,0,2:T(8,128)S(1)} %fusion.1) | data formatting | bytes 524288 | tf_op jit(solution)/shard_map/add | solution.py:120
  62.8 0.6 dynamic-slice
  64.0 0.2 slice_reduce_fusion.1
  64.2 0.2 slice_reduce_fusion
  64.4 10.6 %all-reduce = f32[16]{0:T(128)S(1)} all-reduce(f32[16]{0:T(128)S(1)} %add.84), channel_id=3, replica_groups=mesh['blk'=8,'off'=4] {'off'}, use_global_device_ids=true, to_apply=%region_6.7.clone | all-reduce | flops 16 | bytes 128
  75.0 0.6 fusion.33
  75.6 7.2 %reduce-scatter.2.cloned.1.call-done = f32[4,32,128]{2,1,0:T(8,128)} async-done(((f32[16,32,128]{2,1,0:T(8,128)}), f32[4,32,128]{2,1,0:T(8,128)}) %reduce-scatter.2.cloned.1.call-update) | async-done | bytes 65552 | tf_op jit(solution)/shard_map/reduce_scatter | solution.py:123
  82.8 1.5 %broadcast_divide_fusion = f32[4,32,128]{2,1,0:T(8,128)} fusion(f32[4,32,128]{2,1,0:T(8,128)} %reduce-scatter.2.cloned.1.call-done, f32[4]{0:T(128)S(1)} %get-tuple-element.5), kind=kLoop, calls=%fused_computation.48 | loop fusion | flops 16384 | bytes 131088 | tf_op jit(solution)/shard_map/div | solution.py:126
  (28 shorter events, 1.4 us)
Async XLA Ops:
  7.2 75.7 %reduce-scatter.2.cloned.1.call-start = ((), (), s32[]{:S(2)}) async-start(), calls=%async_computation.1 | async-start | bytes 327680 | tf_op jit(solution)/shard_map/reduce_scatter | solution.py:123
  32.8 3.7 %collective-permute-start = (bf16[16,32,128]{2,1,0:T(8,128)(2,1)S(1)}, bf16[16,32,128]{2,1,0:T(8,128)(2,1)S(1)}, u32[]{:S(2)}, u32[]{:S(2)}) collective-permute-start(bf16[16,32,128]{2,1,0:T(8,128)(2,1)S(1)} %copy.18), channel_id=1, source_target_pairs={{0,28},{4,0},{8,4},{12,8},{16,12},{20,16},{24,20},{28,24},{1,29},{... | collective-permute-start | bytes 393224 | tf_op jit(solution)/shard_map/ppermute | solution.py:13
  36.5 6.0 %collective-permute-start.1 = (bf16[16,32,128]{2,1,0:T(8,128)(2,1)S(1)}, bf16[16,32,128]{2,1,0:T(8,128)(2,1)S(1)}, u32[]{:S(2)}, u32[]{:S(2)}) collective-permute-start(bf16[16,32,128]{2,1,0:T(8,128)(2,1)S(1)} %collective-permute-done), channel_id=1, source_target_pairs={{0,24},{4,28},{8,0},{12,4},{16,8},{20,12},{24,16},{28,20},{1,25},{... | collective-permute-start | bytes 393224 | tf_op jit(solution)/shard_map/ppermute | solution.py:13
  42.5 5.2 %collective-permute-start.2 = (bf16[16,32,128]{2,1,0:T(8,128)(2,1)S(1)}, bf16[16,32,128]{2,1,0:T(8,128)(2,1)S(1)}, u32[]{:S(2)}, u32[]{:S(2)}) collective-permute-start(bf16[16,32,128]{2,1,0:T(8,128)(2,1)S(1)} %broadcast_select_fusion), channel_id=1, source_target_pairs={{0,16},{4,20},{8,24},{12,28},{16,0},{20,4},{24,8},{28,12},{1,17},{... | collective-permute-start | bytes 393224 | tf_op jit(solution)/shard_map/ppermute | solution.py:13
  48.0 6.8 %collective-permute-start.3 = (bf16[16,32,128]{2,1,0:T(8,128)(2,1)S(1)}, bf16[16,32,128]{2,1,0:T(8,128)(2,1)S(1)}, u32[]{:S(2)}, u32[]{:S(2)}) collective-permute-start(bf16[16,32,128]{2,1,0:T(8,128)(2,1)S(1)} %get-tuple-element.7), channel_id=1, source_target_pairs={{0,4},{4,8},{8,12},{12,16},{16,20},{20,24},{24,28},{28,0},{1,5},{5... | collective-permute-start | bytes 393224 | tf_op jit(solution)/shard_map/ppermute | solution.py:13
  59.9 1.2 %copy-start = (f32[128,32,16]{1,2,0:T(8,128)S(1)}, f32[128,32,16]{1,2,0:T(8,128)}, u32[]{:S(2)}) copy-start(f32[128,32,16]{1,2,0:T(8,128)} %fusion.40) | copy-start | bytes 786436
  59.9 1.3 %copy-start.1 = (bf16[16,16,128]{1,0,2:T(8,128)(2,1)S(1)}, bf16[16,16,128]{1,0,2:T(8,128)(2,1)}, u32[]{:S(2)}) copy-start(bf16[16,16,128]{1,0,2:T(8,128)(2,1)} %copy.24) | copy-start | bytes 196612
  61.6 1.2 %copy-start.2 = (u32[32]{0:T(128)S(1)}, u32[32]{0:T(128)}, u32[]{:S(2)}) copy-start(u32[32]{0:T(128)} %constant.70) | copy-start | bytes 388
Sparse Core Ops, SparseCore 0:
  62.9 19.8 reduce-scatter.1
where the time goes:
time: 91.5 us; the launch traced here: 91.2 us
  blocking collectives  34 us (37%)
  waiting for transfers between devices  18.7 us (20%)
  between operations  15 us (16%)
  local copies, waits for them, and re-layouts  10.9 us (12%)
  matrix products  5.46 us (6%)
  other arithmetic  4.18 us (5%)
  starting transfers between devices  3.05 us (3%)
    all_gather x1, blocking collectives, body(): own_block = lax.all_gather(coefficients, 'off', axis=1, tiled=True)  23.4 us
    ppermute x4, waiting for transfers between devices, shifted(): lax.ppermute(array, axis, [(i, (i + by) % count) for i in range(count)])  11.4 us
    unnamed x1, blocking collectives  10.6 us
    reduce_scatter x1, waiting for transfers between devices, body(): lax.psum_scatter(filtered, 'off', scatter_dimension=0, tiled=True)  7.22 us
    ppermute x4, starting transfers between devices, shifted(): lax.ppermute(array, axis, [(i, (i + by) % count) for i in range(count)])  3.02 us
    unnamed x8, local copies, waits for them, and re-layouts  2.54 us
  transfers between devices with their start and end apart: 5, of which 4 were waited for; matrix products, arithmetic and copies ran while one was open for 10% of the time, Pallas kernels for 0%

commit v1 on v0

--- a/solution.py
+++ b/solution.py
@@ -1,3 +1,4 @@
+import functools
 import math
 import jax
 import jax.numpy as jnp
@@ -6,6 +7,21 @@
 
 epsilon = 1e-06
 concentration = 40.0
+
+
+def _refer_rails(in_array, axis_key, axis_k):
+    devs = lax.axis_size(axis_key)
+    piece_now = [(ix - 1, ix) for ix in range(1, devs)] + [(devs - 1, 0)]
+    last = in_array
+    block_list = [last]
+    for _ in range(devs - 1):
+        last = lax.ppermute(last, axis_name=axis_key, perm=piece_now)
+        block_list += [last]
+    kept_arr = jnp.concatenate([*reversed(block_list)], axis=axis_k)
+    return jnp.roll(kept_arr, (lax.axis_index(axis_key) + 1) * last.shape[axis_k], axis=axis_k)
+
+
+build_the_leaf = functools.partial(_refer_rails, axis_key="off", axis_k=1)
 
 
 def shifted(array, axis, by):
@@ -71,7 +87,7 @@
 
 
 def body(coefficients):
-    own_block = lax.all_gather(coefficients, "off", axis=1, tiled=True)
+    own_block = build_the_leaf(coefficients)
     own_inverse = inverse_norms(own_block)
     row_count, radial, angular = own_block.shape
     forward, backward = angle_tables(angular)

time: 91.5 us -> 139 us (1.52)
  waiting for transfers between devices: 18.7 us -> 82.8 us
  blocking collectives: 34 us -> 8.53 us
  local copies, waits for them, and re-layouts: 10.9 us -> 16 us
  starting transfers between devices: 3.05 us -> 5.8 us
  other arithmetic: 4.18 us -> 5.66 us
    ppermute x0 -> x3, waiting for transfers between devices: none -> 42.8 us  [_refer_rails(): last = lax.ppermute(last, axis_name=axis_key, perm=piece_now)]
    all_gather x1 -> x0, blocking collectives: 23.4 us -> none  [body(): own_block = lax.all_gather(coefficients, 'off', axis=1, tiled=True)]
    ppermute x4, waiting for transfers between devices: 11.4 us -> 32.9 us  [shifted(): lax.ppermute(array, axis, [(i, (i + by) % count) for i in range(count)])]
    concatenate x2 -> x1, local copies, waits for them, and re-layouts: 0.86 us -> 5.3 us  [_refer_rails(): jnp.roll(kept_arr, (lax.axis_index(axis_key) + 1) * last.shape[axis_k], a...]
    ppermute x0 -> x3, starting transfers between devices: none -> 3.08 us  [_refer_rails(): last = lax.ppermute(last, axis_name=axis_key, perm=piece_now)]
    unnamed x1, blocking collectives: 10.6 us -> 8.53 us
  transfers between devices with their start and end apart: 5 -> 8, of which waited for: 4 -> 8; matrix products, arithmetic and copies ran while one was open for 10% -> 8% of each run, Pallas kernels for 0% -> 0%
where the time goes in v1:
time: 139 us
  waiting for transfers between devices  82.8 us (60%)
  local copies, waits for them, and re-layouts  16 us (12%)
  between operations  14.9 us (11%)
  blocking collectives  8.53 us (6%)
  starting transfers between devices  5.8 us (4%)
  other arithmetic  5.66 us (4%)
  matrix products  5.34 us (4%)
    ppermute x3, waiting for transfers between devices, _refer_rails(): last = lax.ppermute(last, axis_name=axis_key, perm=piece_now)  42.8 us
    ppermute x4, waiting for transfers between devices, shifted(): lax.ppermute(array, axis, [(i, (i + by) % count) for i in range(count)])  32.9 us
    unnamed x1, blocking collectives  8.53 us
    reduce_scatter x1, waiting for transfers between devices, body(): lax.psum_scatter(filtered, 'off', scatter_dimension=0, tiled=True)  7.04 us
    concatenate x1, local copies, waits for them, and re-layouts, _refer_rails(): jnp.roll(kept_arr, (lax.axis_index(axis_key) + 1) * last.shape[axis_k], a...  5.3 us
    unnamed x8, local copies, waits for them, and re-layouts  3.35 us
    ppermute x3, starting transfers between devices, _refer_rails(): last = lax.ppermute(last, axis_name=axis_key, perm=piece_now)  3.08 us
  transfers between devices with their start and end apart: 8, of which 8 were waited for; matrix products, arithmetic and copies ran while one was open for 8% of the time, Pallas kernels for 0%

profile of v1, /device:TPU:0, one launch (start us, length us, event | category | flops | bytes accessed | tf_op | source)
XLA Modules:
  0.0 139.0 jit_solution(1105108783790848639)
XLA Ops:
  7.2 1.2 copy.31
  8.4 3.1 %collective-permute-start = (bf16[16,8,128]{1,0,2:T(8,128)(2,1)S(1)}, bf16[16,8,128]{1,0,2:T(8,128)(2,1)S(1)}, u32[]{:S(2)}, u32[]{:S(2)}) collective-permute-start(bf16[16,8,128]{1,0,2:T(8,128)(2,1)S(1)} %copy.31), channel_id=1, source_target_pairs={{0,1},{1,2},{2,3},{3,0},{4,5},{5,6},{6,7},{7,4},{8,9},{9,10},{10,1... | collective-permute-start | bytes 98312 | tf_op jit(solution)/shard_map/ppermute | solution.py:18
  11.5 13.9 %collective-permute-done = bf16[16,8,128]{1,0,2:T(8,128)(2,1)S(1)} collective-permute-done((bf16[16,8,128]{1,0,2:T(8,128)(2,1)S(1)}, bf16[16,8,128]{1,0,2:T(8,128)(2,1)S(1)}, u32[]{:S(2)}, u32[]{:S(2)}) %collective-permute-start) | collective-permute-done | bytes 32800 | tf_op jit(solution)/shard_map/ppermute | solution.py:18
  25.4 14.9 %collective-permute-done.1 = bf16[16,8,128]{1,0,2:T(8,128)(2,1)S(1)} collective-permute-done((bf16[16,8,128]{1,0,2:T(8,128)(2,1)S(1)}, bf16[16,8,128]{1,0,2:T(8,128)(2,1)S(1)}, u32[]{:S(2)}, u32[]{:S(2)}) %collective-permute-start.1) | collective-permute-done | bytes 32800 | tf_op jit(solution)/shard_map/ppermute | solution.py:18
  40.3 14.0 %collective-permute-done.2 = bf16[16,8,128]{1,0,2:T(8,128)(2,1)S(1)} collective-permute-done((bf16[16,8,128]{1,0,2:T(8,128)(2,1)S(1)}, bf16[16,8,128]{1,0,2:T(8,128)(2,1)S(1)}, u32[]{:S(2)}, u32[]{:S(2)}) %collective-permute-start.2) | collective-permute-done | bytes 32800 | tf_op jit(solution)/shard_map/ppermute | solution.py:18
  54.3 5.3 %concatenate.33 = bf16[16,64,128]{1,0,2:T(8,128)(2,1)S(1)} concatenate(bf16[16,8,128]{1,0,2:T(8,128)(2,1)S(1)} %collective-permute-done.2, bf16[16,8,128]{1,0,2:T(8,128)(2,1)S(1)} %collective-permute-done.1, bf16[16,8,128]{1,0,2:T(8,128)(2,1)S(1)} %collective-permute-done, bf16[16,8,128]{1,0,2:T(8,128)(2,1)S(1)} %copy.31, bf16[16,8,128]{1,0,2:T(8,128)(2,1)S(1)} %collective-permute-done.2, ...), dimensions={1} | concatenate | bytes 524288 | tf_op jit(solution)/shard_map/jit(_roll_dynamic)/concatenate | solution.py:21
  59.6 0.4 multiply_reduce_fusion.2
  60.1 6.7 %collective-permute-done.3 = bf16[16,32,128]{1,0,2:T(8,128)(2,1)S(1)} collective-permute-done((bf16[16,32,128]{1,0,2:T(8,128)(2,1)S(1)}, bf16[16,32,128]{1,0,2:T(8,128)(2,1)S(1)}, u32[]{:S(2)}, u32[]{:S(2)}) %collective-permute-start.3) | collective-permute-done | bytes 131104 | tf_op jit(solution)/shard_map/ppermute | solution.py:29
  66.8 2.0 %collective-permute-start.4 = (bf16[16,32,128]{1,0,2:T(8,128)(2,1)S(1)}, bf16[16,32,128]{1,0,2:T(8,128)(2,1)S(1)}, u32[]{:S(2)}, u32[]{:S(2)}) collective-permute-start(bf16[16,32,128]{1,0,2:T(8,128)(2,1)S(1)} %collective-permute-done.3), channel_id=1, source_target_pairs={{0,24},{4,28},{8,0},{12,4},{16,8},{20,12},{24,16},{28,20},{1,25},{... | collective-permute-start | bytes 393224 | tf_op jit(solution)/shard_map/ppermute | solution.py:29
  68.7 0.1 sine_negate_fusion
  68.9 12.4 %collective-permute-done.4 = bf16[16,32,128]{1,0,2:T(8,128)(2,1)S(1)} collective-permute-done((bf16[16,32,128]{1,0,2:T(8,128)(2,1)S(1)}, bf16[16,32,128]{1,0,2:T(8,128)(2,1)S(1)}, u32[]{:S(2)}, u32[]{:S(2)}) %collective-permute-start.4) | collective-permute-done | bytes 131104 | tf_op jit(solution)/shard_map/ppermute | solution.py:29
  81.3 0.6 collective-permute-start.5
  81.9 13.4 %collective-permute-done.5 = bf16[16,32,128]{1,0,2:T(8,128)(2,1)S(1)} collective-permute-done((bf16[16,32,128]{1,0,2:T(8,128)(2,1)S(1)}, bf16[16,32,128]{1,0,2:T(8,128)(2,1)S(1)}, u32[]{:S(2)}, u32[]{:S(2)}) %collective-permute-start.5) | collective-permute-done | bytes 131104 | tf_op jit(solution)/shard_map/ppermute | solution.py:29
  95.3 0.4 multiply_reduce_fusion.1
  95.8 0.4 convolution_bitcast_fusion.3
  96.2 0.4 convolution_bitcast_fusion.2
  96.6 0.9 slice_subtract_fusion.1
  97.4 1.3 copy.35
  98.7 0.9 slice_add_fusion.1
  99.6 1.3 copy.34
  100.9 0.3 fusion.5
  101.2 0.3 fusion.45
  101.7 0.4 copy.37
  102.2 1.4 fusion.11
  103.6 1.2 copy.36
  104.8 0.4 collective-permute-done.6
  105.3 0.4 convolution_bitcast_fusion
  105.7 0.3 copy.39
  106.0 0.4 convolution_bitcast_fusion.1
  106.5 0.3 copy.38
  106.8 0.3 multiply_reduce_fusion
  107.1 0.3 fusion.9
  107.4 0.3 fusion.44
  107.9 0.4 copy.41
  108.3 0.4 fusion.10
  108.8 0.4 copy.40
  109.3 0.4 convolution_add_fusion
  109.7 0.8 copy-done
  110.6 0.4 fusion.1
  111.0 1.1 copy.42
  112.2 0.6 copy-done.2
  112.8 0.6 dynamic-slice
  114.0 0.2 slice_reduce_fusion.1
  114.2 0.2 slice_reduce_fusion
  114.5 8.5 %all-reduce = f32[16]{0:T(128)S(1)} all-reduce(f32[16]{0:T(128)S(1)} %add.100), channel_id=3, replica_groups=mesh['blk'=8,'off'=4] {'off'}, use_global_device_ids=true, to_apply=%region_6.7.clone | all-reduce | flops 16 | bytes 128
  123.0 0.6 fusion.39
  123.6 7.0 %reduce-scatter.2.cloned.1.call-done = f32[4,32,128]{2,1,0:T(8,128)} async-done(((f32[16,32,128]{2,1,0:T(8,128)}), f32[4,32,128]{2,1,0:T(8,128)}) %reduce-scatter.2.cloned.1.call-update) | async-done | bytes 65552 | tf_op jit(solution)/shard_map/reduce_scatter | solution.py:139
  130.6 1.5 %broadcast_divide_fusion = f32[4,32,128]{2,1,0:T(8,128)} fusion(f32[4,32,128]{2,1,0:T(8,128)} %reduce-scatter.2.cloned.1.call-done, f32[4]{0:T(128)S(1)} %get-tuple-element.5), kind=kLoop, calls=%fused_computation.50 | loop fusion | flops 16384 | bytes 131088 | tf_op jit(solution)/shard_map/div | solution.py:142
  (27 shorter events, 1.2 us)
Async XLA Ops:
  7.2 123.5 %reduce-scatter.2.cloned.1.call-start = ((), (), s32[]{:S(2)}) async-start(), calls=%async_computation.1 | async-start | bytes 327680 | tf_op jit(solution)/shard_map/reduce_scatter | solution.py:139
  8.4 17.0 %collective-permute-start = (bf16[16,8,128]{1,0,2:T(8,128)(2,1)S(1)}, bf16[16,8,128]{1,0,2:T(8,128)(2,1)S(1)}, u32[]{:S(2)}, u32[]{:S(2)}) collective-permute-start(bf16[16,8,128]{1,0,2:T(8,128)(2,1)S(1)} %copy.31), channel_id=1, source_target_pairs={{0,1},{1,2},{2,3},{3,0},{4,5},{5,6},{6,7},{7,4},{8,9},{9,10},{10,1... | collective-permute-start | bytes 98312 | tf_op jit(solution)/shard_map/ppermute | solution.py:18
  25.4 14.9 %collective-permute-start.1 = (bf16[16,8,128]{1,0,2:T(8,128)(2,1)S(1)}, bf16[16,8,128]{1,0,2:T(8,128)(2,1)S(1)}, u32[]{:S(2)}, u32[]{:S(2)}) collective-permute-start(bf16[16,8,128]{1,0,2:T(8,128)(2,1)S(1)} %collective-permute-done), channel_id=1, source_target_pairs={{0,1},{1,2},{2,3},{3,0},{4,5},{5,6},{6,7},{7,4},{8,9},{9,10},{10,1... | collective-permute-start | bytes 98312 | tf_op jit(solution)/shard_map/ppermute | solution.py:18
  40.3 14.0 %collective-permute-start.2 = (bf16[16,8,128]{1,0,2:T(8,128)(2,1)S(1)}, bf16[16,8,128]{1,0,2:T(8,128)(2,1)S(1)}, u32[]{:S(2)}, u32[]{:S(2)}) collective-permute-start(bf16[16,8,128]{1,0,2:T(8,128)(2,1)S(1)} %collective-permute-done.1), channel_id=1, source_target_pairs={{0,1},{1,2},{2,3},{3,0},{4,5},{5,6},{6,7},{7,4},{8,9},{9,10},{10,1... | collective-permute-start | bytes 98312 | tf_op jit(solution)/shard_map/ppermute | solution.py:18
  60.0 6.8 %collective-permute-start.3 = (bf16[16,32,128]{1,0,2:T(8,128)(2,1)S(1)}, bf16[16,32,128]{1,0,2:T(8,128)(2,1)S(1)}, u32[]{:S(2)}, u32[]{:S(2)}) collective-permute-start(bf16[16,32,128]{1,0,2:T(8,128)(2,1)S(1)} %get-tuple-element.9), channel_id=1, source_target_pairs={{0,28},{4,0},{8,4},{12,8},{16,12},{20,16},{24,20},{28,24},{1,29},{... | collective-permute-start | bytes 393224 | tf_op jit(solution)/shard_map/ppermute | solution.py:29
  66.8 14.5 %collective-permute-start.4 = (bf16[16,32,128]{1,0,2:T(8,128)(2,1)S(1)}, bf16[16,32,128]{1,0,2:T(8,128)(2,1)S(1)}, u32[]{:S(2)}, u32[]{:S(2)}) collective-permute-start(bf16[16,32,128]{1,0,2:T(8,128)(2,1)S(1)} %collective-permute-done.3), channel_id=1, source_target_pairs={{0,24},{4,28},{8,0},{12,4},{16,8},{20,12},{24,16},{28,20},{1,25},{... | collective-permute-start | bytes 393224 | tf_op jit(solution)/shard_map/ppermute | solution.py:29
  81.3 14.0 %collective-permute-start.5 = (bf16[16,32,128]{1,0,2:T(8,128)(2,1)S(1)}, bf16[16,32,128]{1,0,2:T(8,128)(2,1)S(1)}, u32[]{:S(2)}, u32[]{:S(2)}) collective-permute-start(bf16[16,32,128]{1,0,2:T(8,128)(2,1)S(1)} %broadcast_select_fusion), channel_id=1, source_target_pairs={{0,16},{4,20},{8,24},{12,28},{16,0},{20,4},{24,8},{28,12},{1,17},{... | collective-permute-start | bytes 393224 | tf_op jit(solution)/shard_map/ppermute | solution.py:29
  95.7 9.6 %collective-permute-start.6 = (bf16[16,32,128]{1,0,2:T(8,128)(2,1)S(1)}, bf16[16,32,128]{1,0,2:T(8,128)(2,1)S(1)}, u32[]{:S(2)}, u32[]{:S(2)}) collective-permute-start(bf16[16,32,128]{1,0,2:T(8,128)(2,1)S(1)} %get-tuple-element.7), channel_id=1, source_target_pairs={{0,4},{4,8},{8,12},{12,16},{16,20},{20,24},{24,28},{28,0},{1,5},{5... | collective-permute-start | bytes 393224 | tf_op jit(solution)/shard_map/ppermute | solution.py:29
  109.2 1.2 copy-start
  109.3 1.3 copy-start.1
  112.1 0.7 copy-start.2
Sparse Core Ops, SparseCore 0:
  112.3 18.3 reduce-scatter.1
